TPU v7x, 256 devices: a whole 4x4x8 slice. The times are simulated.
256 devices in a mesh: mp: 4 (over y), nodes: 64 (over z, x, core).
Axes of the slice: x: 4, y: 4, z: 8, core: 2. Of those that a mesh axis runs over, the one named last changes fastest.
Arguments:
- grid_latent: float32 [131072, 512], P('nodes'), may hold values from -6 to 6
- mesh_latent: float32 [8192, 512], P('nodes'), may hold values from -250 to 250
- enc_grid_w: float32 [512, 512], P(None, 'mp'), may hold values from -0.25 to 0.25
- enc_mesh_w: float32 [512, 512], P(None, 'mp'), may hold values from -0.25 to 0.25
- enc_out_w: float32 [512, 512], P('mp'), may hold values from -0.25 to 0.25
- block_gain: float32 [512], replicated, may hold values from 0.5 to 1.5
- query_w: float32 [512, 512], P(None, 'mp'), may hold values from -1 to 1
- key_w: float32 [512, 512], P(None, 'mp'), may hold values from -1 to 1
- value_w: float32 [512, 512], P(None, 'mp'), may hold values from -0.25 to 0.25
- out_w: float32 [512, 512], P('mp'), may hold values from -0.25 to 0.25
- up_w: float32 [512, 2048], P(None, 'mp'), may hold values from -0.25 to 0.25
- down_w: float32 [2048, 512], P('mp'), may hold values from -0.125 to 0.125
- dec_gain: float32 [512], replicated, may hold values from 0.5 to 1.5
- dec_grid_w: float32 [512, 512], P(None, 'mp'), may hold values from -0.25 to 0.25
- dec_mesh_w: float32 [512, 512], P(None, 'mp'), may hold values from -0.25 to 0.25
- dec_out_w: float32 [512, 512], P('mp'), may hold values from -0.25 to 0.25
- neighbor_blocks: int32 [64, 16], replicated, may hold values from 0 to 63, as said below
- enc_tiles: int32 [2048, 2], P('nodes'), may hold values from -1 to 1023, as said below
- enc_edges: int32 [2048, 2, 128], P('nodes'), may hold values from 0 to 127
- dec_tiles: int32 [3072, 2], P('nodes'), may hold values from 0 to 1023, as said below
- dec_edges: int32 [3072, 2, 128], P('nodes'), may hold values from 0 to 127
Outputs:
- grid_out: float32 [131072, 512], P('nodes', 'mp')
Inputs may be any that keep to these rules, and one draw needn't show every extreme that they name: `neighbor_blocks`: rows i * 1 to (i + 1) - 1 are the query blocks of index i of nodes; among all entries of those rows, the blocks of any one index j of nodes (ids j * 1 to (j + 1) - 1) are named at most 1 times, and for every i some j is named exactly 1 times. Entries may repeat. `enc_tiles`: tile slots i * 32 to (i + 1) * 32 - 1 belong to index i of nodes; a live tile names a grid block and a mesh block both of index i; an unused slot holds -1 in both columns; on each index the live slots come first, their number differs between indices, and some index has all 32 slots live. `dec_tiles`: tiles i * 48 to (i + 1) * 48 - 1 belong to index i of nodes; each names a grid block of index i and a mesh block of index i - 1, i or i + 1 of nodes (counted around the axis).
All inputs are finite; a program needn't handle non-finite values.
Results may differ from a plain program's by a relative error of at most 0.000098.
Values sent between devices are 32-bit elements; how exact they have to be, the bound alone decides.
A program may use at most 128 MiB of HBM per device.

v0:
```python
import math
import jax
import jax.numpy as jnp
from jax import lax
from jax.sharding import PartitionSpec as P

HEAD_DIM = 128
NODE_BLOCK = 128
FULL_PRECISION = lax.Precision.HIGHEST


def copy_for_each(shard, axis):
    devices = lax.axis_size(axis)
    return lax.all_to_all(
        jnp.broadcast_to(shard[None], (devices, *shard.shape)), axis, 0, 0, tiled=True
    )


def taken_together(shard, axis):
    everything = copy_for_each(shard, axis)
    return jnp.sum(everything, axis=0)


def padded(shard, sides, width):
    for axis, dim in sides:
        devices, length = (lax.axis_size(axis), shard.shape[dim])
        up = [(i, (i + 1) % devices) for i in range(devices)]
        down = [(j, i) for i, j in up]
        last = lax.slice_in_dim(shard, length - width, length, axis=dim)
        initial = lax.slice_in_dim(shard, 0, width, axis=dim)
        before = lax.ppermute(last, axis, up)
        after = lax.ppermute(initial, axis, down)
        shard = jnp.concatenate([before, shard, after], axis=dim)
    return shard


def product(matrix, weight):
    return jnp.dot(matrix, weight, precision=FULL_PRECISION, preferred_element_type=jnp.float32)


def layer_norm(inputs, scales):
    centre = jnp.mean(inputs, axis=-1, keepdims=True)
    shifted = inputs - centre
    spread = jnp.mean(shifted * shifted, axis=-1, keepdims=True)
    return shifted * lax.rsqrt(spread + 1e-05) * scales


def edge_pass(
    source_side, target_side, source_block, target_block, edge_ids, tile_live, target_blocks
):
    source = source_block[:, None] * NODE_BLOCK + edge_ids[:, 0, :]
    target = target_block[:, None] * NODE_BLOCK + edge_ids[:, 1, :]
    message = jax.nn.silu(source_side[source] + target_side[target]) * tile_live[:, None, None]
    within = (edge_ids[:, 1, :][:, None, :] == jnp.arange(NODE_BLOCK)[None, :, None]).astype(
        jnp.float32
    )
    tile_sums = jnp.einsum("tne,teh->tnh", within, message, precision=FULL_PRECISION)
    placing = (target_block[None, :] == jnp.arange(target_blocks)[:, None]).astype(jnp.float32)
    summed = jnp.einsum("bt,tnh->bnh", placing, tile_sums, precision=FULL_PRECISION)
    return summed.reshape(target_blocks * NODE_BLOCK, -1)


def per_device(
    grid_latent,
    mesh_latent,
    enc_grid_w,
    enc_mesh_w,
    enc_out_w,
    block_gain,
    query_w,
    key_w,
    value_w,
    out_w,
    up_w,
    down_w,
    dec_gain,
    dec_grid_w,
    dec_mesh_w,
    dec_out_w,
    neighbor_blocks,
    enc_tiles,
    enc_edges,
    dec_tiles,
    dec_edges,
):
    me_node = lax.axis_index("nodes")
    nodes_count = lax.axis_size("nodes")
    grid_rows = grid_latent.shape[0]
    node_rows = mesh_latent.shape[0]
    grid_blocks = grid_rows // NODE_BLOCK
    node_blocks = node_rows // NODE_BLOCK
    grid_enc = product(grid_latent, enc_grid_w)
    mesh_enc = product(mesh_latent, enc_mesh_w)
    tile_live = enc_tiles[:, 0] >= 0
    source_block = jnp.where(tile_live, enc_tiles[:, 0] - me_node * grid_blocks, 0)
    target_block = jnp.where(tile_live, enc_tiles[:, 1] - me_node * node_blocks, 0)
    enc_agg = edge_pass(
        grid_enc,
        mesh_enc,
        source_block,
        target_block,
        enc_edges,
        tile_live.astype(jnp.float32),
        node_blocks,
    )
    enc_total = taken_together(product(enc_agg, enc_out_w), "mp")
    mesh_one = mesh_latent + enc_total
    normed = layer_norm(mesh_one, block_gain)
    queries = product(normed, query_w)
    key_rows = product(normed, key_w)
    value_rows = product(normed, value_w)
    head_cols = queries.shape[1]
    heads_here = head_cols // HEAD_DIM
    key_values = jnp.concatenate([key_rows, value_rows], axis=1)
    query_blocks = queries.reshape(node_blocks, NODE_BLOCK, heads_here, HEAD_DIM)
    own_lists = lax.dynamic_slice_in_dim(neighbor_blocks, me_node * node_blocks, node_blocks, 0)
    key_piece = lax.all_gather(key_values, "nodes", axis=0, tiled=True)
    running_max = jnp.full((node_blocks, heads_here, NODE_BLOCK), -1e30, jnp.float32)
    row_count = key_piece.shape[0]
    piece_block = jnp.arange(row_count) // NODE_BLOCK
    repeats = jnp.sum(
        (own_lists[:, :, None] == piece_block[None, None, :]).astype(jnp.float32), axis=1
    )
    near_keys = key_piece[:, :head_cols].reshape(row_count, heads_here, HEAD_DIM)
    near_values = key_piece[:, head_cols:].reshape(row_count, heads_here, HEAD_DIM)
    scores = jnp.einsum(
        "bqhd,khd->bhqk", query_blocks, near_keys, precision=FULL_PRECISION
    ) / math.sqrt(HEAD_DIM)
    scores = jnp.where((repeats > 0)[:, None, None, :], scores, -1e30)
    new_max = jnp.maximum(running_max, jnp.max(scores, axis=-1))
    weights = jnp.exp(scores - new_max[..., None]) * repeats[:, None, None, :]
    running_sum = jnp.sum(weights, axis=-1)
    running_out = jnp.einsum("bhqk,khd->bhqd", weights, near_values, precision=FULL_PRECISION)
    running_max, running_sum, running_out = (new_max, running_sum, running_out)
    attended = (
        (running_out / running_sum[..., None]).transpose(0, 2, 1, 3).reshape(node_rows, head_cols)
    )
    hidden = jax.nn.silu(product(normed, up_w))
    block_total = taken_together(product(attended, out_w) + product(hidden, down_w), "mp")
    mesh_two = mesh_one + block_total
    mesh_normed = layer_norm(mesh_two, dec_gain)
    all_blocks = node_blocks * nodes_count
    dec_source = (dec_tiles[:, 0] - (me_node - 1) * node_blocks) % all_blocks
    dec_target = dec_tiles[:, 1] - me_node * grid_blocks
    mesh_dec = product(mesh_normed, dec_mesh_w)
    grid_dec = product(grid_latent, dec_grid_w)
    beside_all = padded(mesh_dec, (("nodes", 0),), node_rows)
    every_tile = jnp.ones((dec_tiles.shape[0],), jnp.float32)
    dec_agg = edge_pass(
        beside_all, grid_dec, dec_source, dec_target, dec_edges, every_tile, grid_blocks
    )
    decoded = lax.psum_scatter(product(dec_agg, dec_out_w), "mp", scatter_dimension=1, tiled=True)
    share_cols = decoded.shape[1]
    grid_share = lax.dynamic_slice_in_dim(
        grid_latent, lax.axis_index("mp") * share_cols, share_cols, 1
    )
    return grid_share + decoded


def solution(mesh):
    in_specs = (
        P("nodes", None),
        P("nodes", None),
        P(None, "mp"),
        P(None, "mp"),
        P("mp", None),
        P(),
        P(None, "mp"),
        P(None, "mp"),
        P(None, "mp"),
        P("mp", None),
        P(None, "mp"),
        P("mp", None),
        P(),
        P(None, "mp"),
        P(None, "mp"),
        P("mp", None),
        P(),
        P("nodes", None),
        P("nodes", None, None),
        P("nodes", None),
        P("nodes", None, None),
    )
    out_specs = P("nodes", "mp")
    return jax.shard_map(
        per_device, mesh=mesh, in_specs=in_specs, out_specs=out_specs, check_vma=False
    )
```

profile of v0, /device:TPU:1, one launch (start us, length us, event | category | flops | bytes accessed | tf_op | source)
XLA Modules:
  0.0 320.2 jit_solution(5665436345619726725)
XLA Ops:
  6.5 0.8 convert_bitcast_fusion
  7.3 0.8 multiply_bitcast_fusion.1
  8.1 0.9 fusion.91
  8.9 5.2 %fusion.94 = f32[2048,128]{1,0:T(8,128)S(1)} fusion(f32[2048,512]{1,0:T(8,128)} %param.21, f32[512,128]{1,0:T(8,128)} %param.23), kind=kOutput, calls=%fused_computation.123 | convolution fusion | flops 1610612736 | bytes 5505024 | tf_op jit(solution)/shard_map/dot_general | solution.py:38
  14.3 14.1 %gather_fusion = f32[4096,128]{1,0:T(8,128)} fusion(f32[2048,128]{1,0:T(8,128)S(1)} %fusion.94, s32[4096]{0:T(1024)S(1)} %get-tuple-element.20), kind=kCustom, calls=%fused_computation | custom fusion | bytes 4210688 | tf_op jit(solution)/shard_map/gather | solution.py:53
  28.4 0.4 fusion.95
  28.8 14.1 %gather_fusion.1 = f32[4096,128]{1,0:T(8,128)} fusion(f32[128,128]{1,0:T(8,128)S(1)} %fusion.95, s32[4096]{0:T(1024)S(1)} %get-tuple-element.21), kind=kCustom, calls=%fused_computation.1 | custom fusion | bytes 4210688 | tf_op jit(solution)/shard_map/gather | solution.py:53
  42.9 1.8 add.221
  44.7 1.9 fusion.19
  46.6 2.0 fusion.15
  48.6 0.4 fusion.96
  49.0 0.1 broadcast_in_dim.17
  49.1 19.0 %all_to_all.10 = f32[4,128,512]{2,1,0:T(8,128)S(1)} all-to-all(f32[4,128,512]{2,1,0:T(8,128)S(1)} %broadcast_in_dim.17), channel_id=1, replica_groups=mesh['mp'=4,'nodes'=64] {'mp'}, dimensions={0} | all-to-all | bytes 2097152 | tf_op jit(solution)/shard_map/all_to_all | solution.py:14
  68.1 0.1 reduce_sum.72
  68.2 1.1 fusion.89
  69.4 0.2 multiply_reduce_fusion.1
  69.6 1.6 fusion.87
  71.2 1.6 fusion.86
  72.8 0.7 pad_maximum_fusion.1
  73.5 0.2 dynamic-slice_reduce_fusion
  73.7 0.2 convert_reduce_fusion
  73.9 1.4 fusion.85
  75.3 0.7 fusion.84
  76.0 0.7 fusion.49
  76.8 84.9 %all-gather.2.cloned.1.call-done = f32[8192,256]{0,1:T(8,128)} async-done(((f32[128,256]{0,1:T(8,128)}), f32[8192,256]{0,1:T(8,128)}) %all-gather.2.cloned.1.call-update) | async-done | bytes 8388624 | tf_op jit(solution)/shard_map/all_gather | solution.py:117
  161.6 10.2 %fusion.92 = (f32[128]{0:T(128)S(1)}, f32[1,8192,1,128]{3,1,2,0:T(8,128)S(1)}) fusion(f32[128,128]{1,0:T(8,128)S(1)} %fusion.85, f32[8192,256]{0,1:T(8,128)} %all-gather.2.cloned.1.call-done, pred[8192]{0:T(1024)(128)(4,1)S(1)} %broadcast_compare_fusion), kind=kOutput, calls=%fused_computation.121 | convolution fusion | flops 1613758336 | bytes 8462848 | tf_op jit(solution)/shard_map/bqhd,khd->bhqk/dot_general | solution.py:126
  171.8 3.5 %fusion.6 = f32[128]{0:T(128)S(1)} fusion(f32[1,8192,1,128]{3,1,2,0:T(8,128)S(1)} %get-tuple-element.19, f32[8192]{0:T(1024)S(1)} %convert_reduce_fusion, f32[128]{0:T(128)S(1)} %broadcast_maximum_fusion), kind=kLoop, calls=%fused_computation.12 | loop fusion | flops 3145600 | bytes 4228096 | tf_op jit(solution)/shard_map/reduce_sum | solution.py:132
  175.3 5.0 %fusion.38 = f32[128,128]{0,1:T(8,128)S(1)} fusion(f32[1,8192,1,128]{3,1,2,0:T(8,128)S(1)} %get-tuple-element.19, f32[8192]{0:T(1024)S(1)} %convert_reduce_fusion, f32[128]{0:T(128)S(1)} %broadcast_maximum_fusion, f32[8192,256]{0,1:T(8,128)S(1)} %copy-done.1, f32[128]{0:T(128)S(1)} %fusion.6), kind=kOutput, calls=%fused_computation.39 | convolution fusion | flops 1612726272 | bytes 8487936 | tf_op jit(solution)/shard_map/bhqk,khd->bhqd/dot_general | solution.py:133
  180.4 0.4 convolution_add_fusion
  180.8 1.1 broadcast_in_dim.21
  181.9 4.0 %all-to-all-start.1 = ((f32[4,128,512]{2,1,0:T(8,128)}), f32[4,128,512]{2,1,0:T(8,128)S(1)}, u32[]{:S(2)}, u32[]{:S(2)}) async-start(f32[4,128,512]{2,1,0:T(8,128)} %broadcast_in_dim.21), calls=%async_computation.1 | async-start | bytes 2097152 | tf_op jit(solution)/shard_map/all_to_all | solution.py:14
  186.0 5.2 %fusion.97 = f32[2048,128]{1,0:T(8,128)S(1)} fusion(f32[2048,512]{1,0:T(8,128)} %param.21, f32[512,128]{1,0:T(8,128)} %param.34), kind=kOutput, calls=%fused_computation.126 | convolution fusion | flops 1610612736 | bytes 5505024 | tf_op jit(solution)/shard_map/dot_general | solution.py:38
  191.2 9.3 %all-to-all-done.1 = f32[4,128,512]{2,1,0:T(8,128)S(1)} async-done(((f32[4,128,512]{2,1,0:T(8,128)}), f32[4,128,512]{2,1,0:T(8,128)S(1)}, u32[]{:S(2)}, u32[]{:S(2)}) %all-to-all-start.1) | async-done | bytes 1048608 | tf_op jit(solution)/shard_map/all_to_all | solution.py:14
  200.6 0.8 reduce_sum.77
  201.4 1.1 fusion.88
  202.4 0.2 multiply_reduce_fusion
  202.6 1.4 fusion.46
  204.0 3.1 collective-permute-start
  207.1 0.1 fusion.64
  207.2 20.9 %gather_fusion.3 = f32[6144,128]{1,0:T(8,128)} fusion(f32[2048,128]{1,0:T(8,128)S(1)} %fusion.97, s32[6144]{0:T(1024)S(1)} %get-tuple-element.23), kind=kCustom, calls=%fused_computation.3 | custom fusion | bytes 6316032 | tf_op jit(solution)/shard_map/gather | solution.py:53
  228.1 20.9 %gather_fusion.2 = f32[6144,128]{1,0:T(8,128)} fusion(f32[384,128]{1,0:T(8,128)S(1)} %pad_maximum_fusion, s32[6144]{0:T(1024)S(1)} %get-tuple-element.22), kind=kCustom, calls=%fused_computation.2 | custom fusion | bytes 6316032 | tf_op jit(solution)/shard_map/gather | solution.py:53
  249.1 3.2 add.222
  252.2 2.9 fusion.9
  255.2 2.9 fusion.7
  258.1 0.3 copy.30
  258.5 4.9 %fusion.98 = f32[2048,512]{1,0:T(8,128)} fusion(f32[2048,128]{1,0:T(8,128)S(1)} %bitcast.97, f32[128,512]{1,0:T(8,128)S(1)} %copy-done.8), kind=kOutput, calls=%fused_computation.127 | convolution fusion | flops 1610612736 | bytes 5505024 | tf_op jit(solution)/shard_map/dot_general | solution.py:38
  263.4 47.3 %reduce-scatter.2.cloned.1.call-done = f32[2048,128]{1,0:T(8,128)} async-done(((f32[2048,512]{1,0:T(8,128)}), f32[2048,128]{1,0:T(8,128)}) %reduce-scatter.2.cloned.1.call-update) | async-done | bytes 1048592 | tf_op jit(solution)/shard_map/reduce_scatter | solution.py:152
  310.7 2.6 dynamic-slice_add_fusion
  (48 shorter events, 0.3 us)
Async XLA Ops:
  6.5 68.7 %copy-start = (f32[512,512]{1,0:T(8,128)S(1)}, f32[512,512]{1,0:T(8,128)}, u32[]{:S(2)}) copy-start(f32[512,512]{1,0:T(8,128)} %param.31) | copy-start | bytes 3145732
  6.5 155.1 %all-gather.2.cloned.1.call-start = ((), (), s32[]{:S(2)}) async-start(), calls=%async_computation.3 | async-start | bytes 8519680 | tf_op jit(solution)/shard_map/all_gather | solution.py:117
  14.2 14.1 %copy-start.4 = (f32[128,512]{1,0:T(8,128)S(1)}, f32[128,512]{1,0:T(8,128)}, u32[]{:S(2)}) copy-start(f32[128,512]{1,0:T(8,128)} %param.22) | copy-start | bytes 786436
  14.3 14.1 %copy-start.5 = (f32[512,128]{1,0:T(8,128)S(1)}, f32[512,128]{1,0:T(8,128)}, u32[]{:S(2)}) copy-start(f32[512,128]{1,0:T(8,128)} %param.24) | copy-start | bytes 786436
  28.8 14.1 %copy-start.2 = (f32[4096,128]{1,0:T(8,128)S(1)}, f32[4096,128]{1,0:T(8,128)}, u32[]{:S(2)}) copy-start(f32[4096,128]{1,0:T(8,128)} %gather_fusion) | copy-start | bytes 6291460
  44.7 1.9 copy-start.12
  44.7 3.9 %copy-start.6 = (f32[128,512]{1,0:T(8,128)S(1)}, f32[128,512]{1,0:T(8,128)}, u32[]{:S(2)}) copy-start(f32[128,512]{1,0:T(8,128)} %param.25) | copy-start | bytes 786436
  48.6 21.0 %copy-start.10 = (f32[512]{0:T(512)S(1)}, f32[512]{0:T(512)}, u32[]{:S(2)}) copy-start(f32[512]{0:T(512)} %param.26) | copy-start | bytes 6148
  49.1 24.4 %copy-start.11 = (s32[64,16]{0,1:T(8,128)S(1)}, s32[64,16]{0,1:T(8,128)}, u32[]{:S(2)}) copy-start(s32[64,16]{0,1:T(8,128)} %param.37) | copy-start | bytes 12292
  68.1 7.9 %copy-start.3 = (f32[512,512]{1,0:T(8,128)S(1)}, f32[512,512]{1,0:T(8,128)}, u32[]{:S(2)}) copy-start(f32[512,512]{1,0:T(8,128)} %param.32) | copy-start | bytes 3145732
  161.6 13.7 %copy-start.1 = (f32[8192,256]{0,1:T(8,128)S(1)}, f32[8192,256]{0,1:T(8,128)}, u32[]{:S(2)}) copy-start(f32[8192,256]{0,1:T(8,128)} %all-gather.2.cloned.1.call-done) | copy-start | bytes 25165828
  175.3 5.0 %copy-start.7 = (f32[128,512]{1,0:T(8,128)S(1)}, f32[128,512]{1,0:T(8,128)}, u32[]{:S(2)}) copy-start(f32[128,512]{1,0:T(8,128)} %param.30) | copy-start | bytes 786436
  180.3 5.6 %copy-start.14 = (s32[48,2]{0,1:T(2,128)S(1)}, s32[48,2]{0,1:T(2,128)}, u32[]{:S(2)}) copy-start(s32[48,2]{0,1:T(2,128)} %param.40) | copy-start | bytes 1156
  180.4 5.6 %copy-start.9 = (s32[48,2,128]{2,1,0:T(2,128)S(1)}, s32[48,2,128]{2,1,0:T(2,128)}, u32[]{:S(2)}) copy-start(s32[48,2,128]{2,1,0:T(2,128)} %param.41) | copy-start | bytes 147460
  181.9 18.7 %all-to-all-start.1 = ((f32[4,128,512]{2,1,0:T(8,128)}), f32[4,128,512]{2,1,0:T(8,128)S(1)}, u32[]{:S(2)}, u32[]{:S(2)}) async-start(f32[4,128,512]{2,1,0:T(8,128)} %broadcast_in_dim.21), calls=%async_computation.1 | async-start | bytes 2097152 | tf_op jit(solution)/shard_map/all_to_all | solution.py:14
  185.9 124.8 %reduce-scatter.2.cloned.1.call-start = ((), (), s32[]{:S(2)}) async-start(), calls=%async_computation.4 | async-start | bytes 5242880 | tf_op jit(solution)/shard_map/reduce_scatter | solution.py:152
  186.0 16.6 %copy-start.13 = (f32[512]{0:T(512)S(1)}, f32[512]{0:T(512)}, u32[]{:S(2)}) copy-start(f32[512]{0:T(512)} %param.33) | copy-start | bytes 6148
  204.0 24.1 %collective-permute-start = (f32[128,128]{1,0:T(8,128)S(1)}, f32[128,128]{1,0:T(8,128)S(1)}, u32[]{:S(2)}, u32[]{:S(2)}) collective-permute-start(f32[128,128]{1,0:T(8,128)S(1)} %fusion.46), channel_id=1, source_target_pairs={{0,1},{1,2},{2,3},{3,4},{4,5},{5,6},{6,7},{7,8},{8,9},{9,10},{10,1... | collective-permute-start | bytes 196616 | tf_op jit(solution)/shard_map/ppermute | solution.py:31
  207.1 21.0 %collective-permute-start.1 = (f32[128,128]{1,0:T(8,128)S(1)}, f32[128,128]{1,0:T(8,128)S(1)}, u32[]{:S(2)}, u32[]{:S(2)}) collective-permute-start(f32[128,128]{1,0:T(8,128)S(1)} %fusion.46), channel_id=1, source_target_pairs={{1,0},{2,1},{3,2},{4,3},{5,4},{6,5},{7,6},{8,7},{9,8},{10,9},{11,1... | collective-permute-start | bytes 196616 | tf_op jit(solution)/shard_map/ppermute | solution.py:32
  255.2 3.3 %copy-start.8 = (f32[128,512]{1,0:T(8,128)S(1)}, f32[128,512]{1,0:T(8,128)}, u32[]{:S(2)}) copy-start(f32[128,512]{1,0:T(8,128)} %param.36) | copy-start | bytes 786436
Sparse Core Ops, SparseCore 0:
  73.6 87.9 all-gather.1
  263.6 47.1 reduce-scatter.1
where the time goes:
time: 321 us; the launch traced here: 320 us
  waiting for transfers between devices  142 us (44%)
  local copies, waits for them, and re-layouts  72.8 us (23%)
  matrix products  48.9 us (15%)
  blocking collectives  19 us (6%)
  other arithmetic  17.1 us (5%)
  between operations  13.8 us (4%)
  starting transfers between devices  7.08 us (2%)
    all_gather x1, waiting for transfers between devices, per_device(): key_piece = lax.all_gather(key_values, 'nodes', axis=0, tiled=True)  84.9 us
    reduce_scatter x1, waiting for transfers between devices, per_device(): lax.psum_scatter(product(dec_agg, dec_out_w), 'mp', scatter_dimension=1,...  47.3 us
    gather x2, local copies, waits for them, and re-layouts, edge_pass(): source_side[source] + target_side[target]  35 us
    gather x2, local copies, waits for them, and re-layouts, edge_pass(): target_side[target]  35 us
    dot_general x12, matrix products, product(): jnp.dot(matrix, weight, precision=FULL_PRECISION, preferred_element_type=...  24 us
    all_to_all x1, blocking collectives, copy_for_each(): lax.all_to_all(jnp.broadcast_to(shard[None], (devices, *shard.shape)), ax...  19 us
    dot_general x1, matrix products, per_device(): jnp.einsum('bqhd,khd->bhqk', query_blocks, near_keys, precision=FULL_PREC...  10.2 us
    all_to_all x1, waiting for transfers between devices, copy_for_each(): lax.all_to_all(jnp.broadcast_to(shard[None], (devices, *shard.shape)), ax...  9.34 us
  transfers between devices with their start and end apart: 5, of which 3 were waited for; matrix products, arithmetic and copies ran while one was open for 9% of the time, Pallas kernels for 0%

commit v1 on v0

--- a/solution.py
+++ b/solution.py
@@ -114,7 +114,10 @@
     key_values = jnp.concatenate([key_rows, value_rows], axis=1)
     query_blocks = queries.reshape(node_blocks, NODE_BLOCK, heads_here, HEAD_DIM)
     own_lists = lax.dynamic_slice_in_dim(neighbor_blocks, me_node * node_blocks, node_blocks, 0)
-    key_piece = lax.all_gather(key_values, "nodes", axis=0, tiled=True)
+    size = lax.axis_size("nodes")
+    tiles = jnp.stack([key_values for _ in range(size)])
+    tiles = lax.all_to_all(tiles, "nodes", split_axis=0, concat_axis=0)
+    key_piece = jnp.concatenate(tiles, axis=0)
     running_max = jnp.full((node_blocks, heads_here, NODE_BLOCK), -1e30, jnp.float32)
     row_count = key_piece.shape[0]
     piece_block = jnp.arange(row_count) // NODE_BLOCK

time: 321 us -> 430 us (1.34)
  waiting for transfers between devices: 142 us -> 232 us
  starting transfers between devices: 7.08 us -> 25.3 us
  local copies, waits for them, and re-layouts: 72.8 us -> 77.2 us
    all_to_all x0 -> x1, waiting for transfers between devices: none -> 180 us  [per_device(): tiles = lax.all_to_all(tiles, 'nodes', split_axis=0, concat_axis=0)]
    all_gather x1 -> x0, waiting for transfers between devices: 84.9 us -> none  [per_device(): key_piece = lax.all_gather(key_values, 'nodes', axis=0, tiled=True)]
    all_to_all x0 -> x1, starting transfers between devices: none -> 13.7 us  [per_device(): tiles = lax.all_to_all(tiles, 'nodes', split_axis=0, concat_axis=0)]
    dot_general x1, matrix products: 5 us -> 10.1 us  [per_device(): jnp.einsum('bhqk,khd->bhqd', weights, near_values, precision=FULL_PRECISION)]
    ppermute x1, starting transfers between devices: 3.07 us -> 8.05 us  [padded(): before = lax.ppermute(last, axis, up)]
  transfers between devices with their start and end apart: 5 -> 5, of which waited for: 3 -> 3; matrix products, arithmetic and copies ran while one was open for 9% -> 7% of each run, Pallas kernels for 0% -> 0%
where the time goes in v1:
time: 430 us; the launch traced here: 429 us
  waiting for transfers between devices  232 us (54%)
  local copies, waits for them, and re-layouts  77.2 us (18%)
  matrix products  47.4 us (11%)
  starting transfers between devices  25.3 us (6%)
  blocking collectives  19 us (4%)
  between operations  13.9 us (3%)
  other arithmetic  13.8 us (3%)
    all_to_all x1, waiting for transfers between devices, per_device(): tiles = lax.all_to_all(tiles, 'nodes', split_axis=0, concat_axis=0)  180 us
    reduce_scatter x1, waiting for transfers between devices, per_device(): lax.psum_scatter(product(dec_agg, dec_out_w), 'mp', scatter_dimension=1,...  47.1 us
    gather x2, local copies, waits for them, and re-layouts, edge_pass(): source_side[source] + target_side[target]  35.1 us
    gather x2, local copies, waits for them, and re-layouts, edge_pass(): target_side[target]  35 us
    dot_general x12, matrix products, product(): jnp.dot(matrix, weight, precision=FULL_PRECISION, preferred_element_type=...  20.2 us
    all_to_all x1, blocking collectives, copy_for_each(): lax.all_to_all(jnp.broadcast_to(shard[None], (devices, *shard.shape)), ax...  19 us
    all_to_all x1, starting transfers between devices, per_device(): tiles = lax.all_to_all(tiles, 'nodes', split_axis=0, concat_axis=0)  13.7 us
    dot_general x1, matrix products, per_device(): jnp.einsum('bhqk,khd->bhqd', weights, near_values, precision=FULL_PRECISION)  10.1 us
  transfers between devices with their start and end apart: 5, of which 3 were waited for; matrix products, arithmetic and copies ran while one was open for 7% of the time, Pallas kernels for 0%

profile of v1, /device:TPU:1, one launch (start us, length us, event | category | flops | bytes accessed | tf_op | source)
XLA Modules:
  0.0 429.0 jit_solution(13545191016786041624)
XLA Ops:
  6.5 0.8 convert_bitcast_fusion
  7.3 0.8 multiply_bitcast_fusion.1
  8.1 0.9 fusion.91
  8.9 5.2 %fusion.94 = f32[2048,128]{1,0:T(8,128)S(1)} fusion(f32[2048,512]{1,0:T(8,128)} %param.21, f32[512,128]{1,0:T(8,128)} %param.23), kind=kOutput, calls=%fused_computation.123 | convolution fusion | flops 1610612736 | bytes 5505024 | tf_op jit(solution)/shard_map/dot_general | solution.py:38
  14.3 14.1 %gather_fusion = f32[4096,128]{1,0:T(8,128)} fusion(f32[2048,128]{1,0:T(8,128)S(1)} %fusion.94, s32[4096]{0:T(1024)S(1)} %get-tuple-element.20), kind=kCustom, calls=%fused_computation | custom fusion | bytes 4210688 | tf_op jit(solution)/shard_map/gather | solution.py:53
  28.4 0.4 fusion.95
  28.8 14.1 %gather_fusion.1 = f32[4096,128]{1,0:T(8,128)} fusion(f32[128,128]{1,0:T(8,128)S(1)} %fusion.95, s32[4096]{0:T(1024)S(1)} %get-tuple-element.21), kind=kCustom, calls=%fused_computation.1 | custom fusion | bytes 4210688 | tf_op jit(solution)/shard_map/gather | solution.py:53
  42.9 1.8 add.221
  44.7 1.9 fusion.19
  46.7 2.0 fusion.15
  48.7 0.4 fusion.96
  49.0 0.1 broadcast_in_dim.17
  49.2 19.0 %all_to_all.15 = f32[4,128,512]{2,1,0:T(8,128)S(1)} all-to-all(f32[4,128,512]{2,1,0:T(8,128)S(1)} %broadcast_in_dim.17), channel_id=1, replica_groups=mesh['mp'=4,'nodes'=64] {'mp'}, dimensions={0} | all-to-all | bytes 2097152 | tf_op jit(solution)/shard_map/all_to_all | solution.py:14
  68.3 0.1 fusion.89
  68.4 0.2 multiply_reduce_fusion.1
  68.6 0.7 fusion.87
  69.3 0.7 fusion.86
  69.9 0.1 copy.31
  70.0 4.2 stack.2
  74.3 13.7 %all-to-all-start.1 = ((f32[64,128,256]{2,1,0:T(8,128)}), f32[64,128,256]{2,1,0:T(8,128)}, u32[]{:S(2)}, u32[]{:S(2)}) async-start(f32[64,128,256]{2,1,0:T(8,128)} %stack.2), calls=%async_computation.1 | async-start | bytes 16777216 | tf_op jit(solution)/shard_map/all_to_all | solution.py:119
  88.0 0.2 dynamic-slice_reduce_fusion
  88.2 0.2 convert_reduce_fusion
  88.4 0.4 fusion.85
  88.8 0.7 fusion.84
  89.6 0.8 fusion.49
  90.3 180.1 %all-to-all-done.1 = f32[64,128,256]{2,1,0:T(8,128)} async-done(((f32[64,128,256]{2,1,0:T(8,128)}), f32[64,128,256]{2,1,0:T(8,128)}, u32[]{:S(2)}, u32[]{:S(2)}) %all-to-all-start.1) | async-done | bytes 8388640 | tf_op jit(solution)/shard_map/all_to_all | solution.py:119
  270.4 7.3 %fusion.92 = (f32[128]{0:T(128)S(1)}, f32[1,8192,1,128]{3,1,2,0:T(8,128)S(1)}) fusion(f32[128,128]{1,0:T(8,128)S(1)} %fusion.85, f32[8192,256]{1,0:T(8,128)} %bitcast.16, pred[8192]{0:T(1024)(128)(4,1)S(1)} %broadcast_compare_fusion), kind=kOutput, calls=%fused_computation.121 | convolution fusion | flops 1613758336 | bytes 8462848 | tf_op jit(solution)/shard_map/bqhd,khd->bhqk/dot_general | solution.py:129
  277.7 3.5 fusion.6
  281.2 10.1 %fusion.38 = f32[128,128]{0,1:T(8,128)S(1)} fusion(f32[1,8192,1,128]{3,1,2,0:T(8,128)S(1)} %get-tuple-element.19, f32[8192]{0:T(1024)S(1)} %convert_reduce_fusion, f32[128]{0:T(128)S(1)} %broadcast_maximum_fusion, f32[8192,256]{1,0:T(8,128)} %bitcast.16, f32[128]{0:T(128)S(1)} %fusion.6), kind=kOutput, calls=%fused_computation.39 | convolution fusion | flops 1612726272 | bytes 8487936 | tf_op jit(solution)/shard_map/bhqk,khd->bhqd/dot_general | solution.py:136
  291.4 0.4 convolution_add_fusion
  291.9 1.1 broadcast_in_dim.21
  293.0 3.5 all-to-all-start.2
  296.6 5.2 %fusion.97 = f32[2048,128]{1,0:T(8,128)S(1)} fusion(f32[2048,512]{1,0:T(8,128)} %param.21, f32[512,128]{1,0:T(8,128)S(1)} %copy-done.12), kind=kOutput, calls=%fused_computation.126 | convolution fusion | flops 1610612736 | bytes 5505024 | tf_op jit(solution)/shard_map/dot_general | solution.py:38
  301.9 5.3 %all-to-all-done.2 = f32[4,128,512]{2,1,0:T(8,128)S(1)} async-done(((f32[4,128,512]{2,1,0:T(8,128)}), f32[4,128,512]{2,1,0:T(8,128)S(1)}, u32[]{:S(2)}, u32[]{:S(2)}) %all-to-all-start.2) | async-done | bytes 1048608 | tf_op jit(solution)/shard_map/all_to_all | solution.py:14
  307.2 0.1 reduce_sum.77
  307.3 0.1 fusion.88
  307.4 0.2 multiply_reduce_fusion
  307.6 0.4 fusion.46
  308.0 8.1 %collective-permute-start = (f32[128,128]{1,0:T(8,128)S(1)}, f32[128,128]{1,0:T(8,128)S(1)}, u32[]{:S(2)}, u32[]{:S(2)}) collective-permute-start(f32[128,128]{1,0:T(8,128)S(1)} %fusion.46), channel_id=1, source_target_pairs={{0,1},{1,2},{2,3},{3,4},{4,5},{5,6},{6,7},{7,8},{8,9},{9,10},{10,1... | collective-permute-start | bytes 196616 | tf_op jit(solution)/shard_map/ppermute | solution.py:31
  316.2 20.9 %gather_fusion.3 = f32[6144,128]{1,0:T(8,128)} fusion(f32[2048,128]{1,0:T(8,128)S(1)} %fusion.97, s32[6144]{0:T(1024)S(1)} %get-tuple-element.23), kind=kCustom, calls=%fused_computation.3 | custom fusion | bytes 6316032 | tf_op jit(solution)/shard_map/gather | solution.py:53
  337.1 21.0 %gather_fusion.2 = f32[6144,128]{1,0:T(8,128)} fusion(f32[384,128]{1,0:T(8,128)S(1)} %pad_maximum_fusion, s32[6144]{0:T(1024)S(1)} %get-tuple-element.22), kind=kCustom, calls=%fused_computation.2 | custom fusion | bytes 6316032 | tf_op jit(solution)/shard_map/gather | solution.py:53
  358.1 3.2 add.222
  361.3 3.0 fusion.9
  364.2 2.9 fusion.7
  367.1 0.3 copy.33
  367.5 4.9 %fusion.98 = f32[2048,512]{1,0:T(8,128)} fusion(f32[2048,128]{1,0:T(8,128)S(1)} %bitcast.98, f32[128,512]{1,0:T(8,128)S(1)} %copy-done.13), kind=kOutput, calls=%fused_computation.127 | convolution fusion | flops 1610612736 | bytes 5505024 | tf_op jit(solution)/shard_map/dot_general | solution.py:38
  372.4 47.1 %reduce-scatter.2.cloned.1.call-done = f32[2048,128]{1,0:T(8,128)} async-done(((f32[2048,512]{1,0:T(8,128)}), f32[2048,128]{1,0:T(8,128)}) %reduce-scatter.2.cloned.1.call-update) | async-done | bytes 1048592 | tf_op jit(solution)/shard_map/reduce_scatter | solution.py:155
  419.5 2.6 dynamic-slice_add_fusion
  (59 shorter events, 0.5 us)
Async XLA Ops:
  6.5 82.3 %copy-start = (f32[512,512]{1,0:T(8,128)S(1)}, f32[512,512]{1,0:T(8,128)}, u32[]{:S(2)}) copy-start(f32[512,512]{1,0:T(8,128)} %param.31) | copy-start | bytes 3145732
  14.3 14.1 %copy-start.4 = (f32[128,512]{1,0:T(8,128)S(1)}, f32[128,512]{1,0:T(8,128)}, u32[]{:S(2)}) copy-start(f32[128,512]{1,0:T(8,128)} %param.22) | copy-start | bytes 786436
  14.3 14.1 %copy-start.5 = (f32[512,128]{1,0:T(8,128)S(1)}, f32[512,128]{1,0:T(8,128)}, u32[]{:S(2)}) copy-start(f32[512,128]{1,0:T(8,128)} %param.24) | copy-start | bytes 786436
  28.8 14.1 %copy-start.2 = (f32[4096,128]{1,0:T(8,128)S(1)}, f32[4096,128]{1,0:T(8,128)}, u32[]{:S(2)}) copy-start(f32[4096,128]{1,0:T(8,128)} %gather_fusion) | copy-start | bytes 6291460
  44.7 1.9 copy-start.17
  44.7 3.9 copy-start.6
  48.6 19.9 %copy-start.7 = (f32[512,128]{1,0:T(8,128)S(1)}, f32[512,128]{1,0:T(8,128)}, u32[]{:S(2)}) copy-start(f32[512,128]{1,0:T(8,128)} %param.28) | copy-start | bytes 786436
  48.7 19.9 %copy-start.15 = (f32[512]{0:T(512)S(1)}, f32[512]{0:T(512)}, u32[]{:S(2)}) copy-start(f32[512]{0:T(512)} %param.26) | copy-start | bytes 6148
  49.0 20.2 %copy-start.8 = (f32[512,128]{1,0:T(8,128)S(1)}, f32[512,128]{1,0:T(8,128)}, u32[]{:S(2)}) copy-start(f32[512,128]{1,0:T(8,128)} %param.29) | copy-start | bytes 786436
  74.3 13.7 %copy-start.16 = (s32[64,16]{0,1:T(8,128)S(1)}, s32[64,16]{0,1:T(8,128)}, u32[]{:S(2)}) copy-start(s32[64,16]{0,1:T(8,128)} %param.37) | copy-start | bytes 12292
  74.3 14.1 %copy-start.9 = (f32[512,128]{1,0:T(8,128)S(1)}, f32[512,128]{1,0:T(8,128)}, u32[]{:S(2)}) copy-start(f32[512,128]{1,0:T(8,128)} %param.27) | copy-start | bytes 786436
  74.3 15.3 %copy-start.3 = (f32[512,512]{1,0:T(8,128)S(1)}, f32[512,512]{1,0:T(8,128)}, u32[]{:S(2)}) copy-start(f32[512,512]{1,0:T(8,128)} %param.32) | copy-start | bytes 3145732
  74.3 196.1 %all-to-all-start.1 = ((f32[64,128,256]{2,1,0:T(8,128)}), f32[64,128,256]{2,1,0:T(8,128)}, u32[]{:S(2)}, u32[]{:S(2)}) async-start(f32[64,128,256]{2,1,0:T(8,128)} %stack.2), calls=%async_computation.1 | async-start | bytes 16777216 | tf_op jit(solution)/shard_map/all_to_all | solution.py:119
  281.2 10.2 %copy-start.10 = (f32[128,512]{1,0:T(8,128)S(1)}, f32[128,512]{1,0:T(8,128)}, u32[]{:S(2)}) copy-start(f32[128,512]{1,0:T(8,128)} %param.30) | copy-start | bytes 786436
  291.4 5.1 %copy-start.19 = (s32[48,2]{0,1:T(2,128)S(1)}, s32[48,2]{0,1:T(2,128)}, u32[]{:S(2)}) copy-start(s32[48,2]{0,1:T(2,128)} %param.40) | copy-start | bytes 1156
  291.4 5.2 %copy-start.14 = (s32[48,2,128]{2,1,0:T(2,128)S(1)}, s32[48,2,128]{2,1,0:T(2,128)}, u32[]{:S(2)}) copy-start(s32[48,2,128]{2,1,0:T(2,128)} %param.41) | copy-start | bytes 147460
  291.4 5.2 %copy-start.12 = (f32[512,128]{1,0:T(8,128)S(1)}, f32[512,128]{1,0:T(8,128)}, u32[]{:S(2)}) copy-start(f32[512,128]{1,0:T(8,128)} %param.34) | copy-start | bytes 786436
  293.0 14.2 %all-to-all-start.2 = ((f32[4,128,512]{2,1,0:T(8,128)}), f32[4,128,512]{2,1,0:T(8,128)S(1)}, u32[]{:S(2)}, u32[]{:S(2)}) async-start(f32[4,128,512]{2,1,0:T(8,128)} %broadcast_in_dim.21), calls=%async_computation.2 | async-start | bytes 2097152 | tf_op jit(solution)/shard_map/all_to_all | solution.py:14
  296.5 123.0 %reduce-scatter.2.cloned.1.call-start = ((), (), s32[]{:S(2)}) async-start(), calls=%async_computation.4 | async-start | bytes 5242880 | tf_op jit(solution)/shard_map/reduce_scatter | solution.py:155
  296.6 11.0 %copy-start.11 = (f32[512,128]{1,0:T(8,128)S(1)}, f32[512,128]{1,0:T(8,128)}, u32[]{:S(2)}) copy-start(f32[512,128]{1,0:T(8,128)} %param.35) | copy-start | bytes 786436
  296.6 11.0 %copy-start.18 = (f32[512]{0:T(512)S(1)}, f32[512]{0:T(512)}, u32[]{:S(2)}) copy-start(f32[512]{0:T(512)} %param.33) | copy-start | bytes 6148
  308.0 29.1 %collective-permute-start = (f32[128,128]{1,0:T(8,128)S(1)}, f32[128,128]{1,0:T(8,128)S(1)}, u32[]{:S(2)}, u32[]{:S(2)}) collective-permute-start(f32[128,128]{1,0:T(8,128)S(1)} %fusion.46), channel_id=1, source_target_pairs={{0,1},{1,2},{2,3},{3,4},{4,5},{5,6},{6,7},{7,8},{8,9},{9,10},{10,1... | collective-permute-start | bytes 196616 | tf_op jit(solution)/shard_map/ppermute | solution.py:31
  316.1 21.0 %collective-permute-start.1 = (f32[128,128]{1,0:T(8,128)S(1)}, f32[128,128]{1,0:T(8,128)S(1)}, u32[]{:S(2)}, u32[]{:S(2)}) collective-permute-start(f32[128,128]{1,0:T(8,128)S(1)} %fusion.46), channel_id=1, source_target_pairs={{1,0},{2,1},{3,2},{4,3},{5,4},{6,5},{7,6},{8,7},{9,8},{10,9},{11,1... | collective-permute-start | bytes 196616 | tf_op jit(solution)/shard_map/ppermute | solution.py:32
  364.2 3.3 copy-start.13
  372.4 49.7 %copy-start.1 = (f32[512,512]{1,0:T(8,128)S(1)}, f32[512,512]{1,0:T(8,128)}, u32[]{:S(2)}) copy-start(f32[512,512]{1,0:T(8,128)} %param.31) | copy-start | bytes 3145732
Sparse Core Ops, SparseCore 0:
  372.6 46.9 reduce-scatter.1
